TPU v7x, 32 devices: a whole 2x2x4 slice. The times are simulated.
32 devices in a mesh: pair: 2 (over x), grow: 4 (over z), gcol: 4 (over y, core).
Axes of the slice: x: 2, y: 2, z: 4, core: 2. Of those that a mesh axis runs over, the one named last changes fastest.
Arguments:
- valence: bfloat16 [2, 64, 128, 16384], P(None, None, ('grow', 'gcol')), may hold values from -6 to 6
- conduction: bfloat16 [2, 2, 128, 16384], P(None, 'pair', ('grow', 'gcol')), may hold values from -6 to 6
- pair_bands: int32 [2, 32], P('pair'), may hold values from 0 to 63, as said below
- e_val: float32 [64], replicated, may hold values from -12 to -1
- e_cond: float32 [2], P('pair'), may hold values from 1 to 12
- g_index: int32 [3840], replicated, may hold values from 0 to 2097151, as said below
- slab_index: int32 [256], replicated, may hold values from 0 to 2097151, as said below
Outputs:
- chi_slab: float32 [2, 3840, 256], P(None, ('pair', 'grow'), 'gcol')
Inputs may be any that keep to these rules, and one draw needn't show every extreme that they name: `pair_bands`: each row lists 32 different valence bands. All entries of g_index and slab_index name different grid points. Write G = ((p * 4 + g) * 4 + c) * 120 + j with j < 120; the grid point of row G has q2 within [c * 32, (c + 1) * 32) and q3 within [b w, (b + 1) w) with b = g * 4 + c and w = 8. `slab_index`: write H = ((c * 2 + p) * 4 + g) * 8 + j with j < 8; the grid point of column H lies in the same range of q2 and q3 as the rows of g_index with these g and c.
All inputs are finite; a program needn't handle non-finite values.
Results may differ from a plain program's by a relative error of at most 0.012.
Values may be sent and summed in bfloat16 or wider, within the bound.
A program may use at most 256 MiB of HBM per device.

v0:
```python
import math

import jax
import jax.numpy as jnp
from jax import lax
from jax.sharding import PartitionSpec as P

NGRID = 128


def transform_table(count, positions):
    freq = jnp.arange(count, dtype=jnp.int32)
    phase = freq[:, None] * positions[None, :] % count
    angle = phase.astype(jnp.float32) * (2.0 * math.pi / count)
    scale = 1.0 / math.sqrt(count)
    cosine = (jnp.cos(angle) * scale).astype(jnp.bfloat16)
    sine = (jnp.sin(angle) * scale).astype(jnp.bfloat16)
    upper = jnp.stack([cosine, sine], axis=1)
    lower = jnp.stack([-sine, cosine], axis=1)
    return jnp.stack([upper, lower])


def on_device(valence, conduction, pair_bands, e_val, e_cond, g_index, slab_index):
    n_pair = lax.axis_size("pair")
    n_grow = lax.axis_size("grow")
    n_gcol = lax.axis_size("gcol")
    grow_at = lax.axis_index("grow")
    gcol_at = lax.axis_index("gcol")
    planes = valence.shape[2]
    bands_here, partners = pair_bands.shape
    pairs_here = bands_here * partners
    total_pairs = pairs_here * n_pair
    picked = jnp.take(valence, pair_bands.reshape(-1), axis=1).astype(jnp.float32)
    cond_rep = jnp.repeat(conduction, partners, axis=1).astype(jnp.float32)
    real_part = picked[0] * cond_rep[0] + picked[1] * cond_rep[1]
    imag_part = picked[0] * cond_rep[1] - picked[1] * cond_rep[0]
    density = jnp.stack([real_part, imag_part]).astype(jnp.bfloat16)
    density = jnp.transpose(density.reshape(2, pairs_here, planes, NGRID, NGRID), (0, 2, 3, 4, 1))
    natural = transform_table(NGRID, jnp.arange(NGRID, dtype=jnp.int32))
    third = jnp.einsum(
        "okix,iabxp->oabkp", natural, density, preferred_element_type=jnp.float32
    ).astype(jnp.bfloat16)
    second = jnp.einsum(
        "okix,iaxbp->oakbp", natural, third, preferred_element_type=jnp.float32
    ).astype(jnp.bfloat16)
    moved = lax.all_to_all(second, ("grow", "gcol"), split_axis=3, concat_axis=1, tiled=True)
    positions = jnp.arange(NGRID, dtype=jnp.int32)
    wide_two = NGRID
    base_three = (grow_at * n_gcol + gcol_at) * planes
    table_first = transform_table(NGRID, positions)
    elements = jnp.einsum(
        "okix,ixabp->okabp", table_first, moved, preferred_element_type=jnp.float32
    ).astype(jnp.bfloat16)
    flat = elements.reshape(2, -1, pairs_here)

    def local_offset(index):
        first_q = index // (NGRID * NGRID)
        second_q = index // NGRID % NGRID
        third_q = index % NGRID
        return (first_q * wide_two + second_q) * planes + third_q - base_three

    row_count = g_index.shape[0] // (n_pair * n_grow * n_gcol)
    row_ids = g_index.reshape(n_pair, n_grow, n_gcol, row_count)[:, grow_at, gcol_at]
    rows = jnp.take(flat, local_offset(row_ids).reshape(-1), axis=1).reshape(
        2, n_pair, row_count, pairs_here
    )
    gaps = jnp.take(e_val, pair_bands) - e_cond[:, None]
    weight = (2.0 / (gaps * math.sqrt(total_pairs))).reshape(-1)
    weighted = (rows.astype(jnp.float32) * weight).astype(jnp.bfloat16)
    col_count = slab_index.shape[0] // (n_pair * n_grow * n_gcol)
    col_ids = slab_index.reshape(n_gcol, n_pair, n_grow, col_count)[gcol_at, :, grow_at]
    cols = jnp.take(flat, local_offset(col_ids).reshape(-1), axis=1).reshape(
        2, n_pair, col_count, pairs_here
    )
    row_block = lax.all_to_all(weighted, "pair", split_axis=1, concat_axis=3, tiled=True).reshape(
        2, row_count, total_pairs
    )
    spread = lax.all_gather(
        cols.reshape(2, n_pair, 1, col_count, pairs_here), "grow", axis=2, tiled=True
    )
    slab = lax.all_gather(spread, "pair", axis=4, tiled=True).reshape(2, -1, total_pairs)
    conjugate = jnp.stack([jnp.stack([slab[0], slab[1]]), jnp.stack([-slab[1], slab[0]])])
    return jnp.einsum(
        "irk,oick->orc",
        lax.all_gather(row_block, "gcol", axis=1, tiled=True),
        conjugate,
        preferred_element_type=jnp.float32,
    )


def solution(mesh):
    in_specs = (
        P(None, None, ("grow", "gcol"), None),
        P(None, "pair", ("grow", "gcol"), None),
        P("pair", None),
        P(),
        P("pair"),
        P(),
        P(),
    )
    out_specs = P(None, ("pair", "grow"), "gcol")
    return jax.shard_map(
        on_device, mesh=mesh, in_specs=in_specs, out_specs=out_specs, check_vma=False
    )
```

profile of v0, /device:TPU:0, one launch (start us, length us, event | category | flops | bytes accessed | tf_op | source)
XLA Modules:
  0.0 696.2 jit_solution(6668681434692969918)
XLA Ops:
  0.0 0.3 multiply_convert_fusion.1
  0.3 0.3 fusion.31
  0.6 0.7 fusion.44
  1.2 0.7 compare_and_fusion.1
  1.9 1.1 convert_element_type.90
  3.1 11.8 %gather_fusion = bf16[32,2,8,16384]{3,2,1,0:T(8,128)(2,1)} fusion(bf16[2,64,8,16384]{3,2,1,0:T(8,128)(2,1)} %param.7, s32[1024]{0:T(1024)S(1)} %pad_clamp_fusion.3), kind=kCustom, calls=%fused_computation | custom fusion | bytes 33554560 | tf_op jit(solution)/shard_map/jit(_take)/gather | solution.py:33
  14.9 18.3 %convert_bitcast_fusion = f32[2,32,8,16384]{3,2,0,1:T(8,128)} fusion(bf16[32,2,8,16384]{3,2,1,0:T(8,128)(2,1)} %gather_fusion, pred[32]{0:T(512)(128)(4,1)S(1)} %compare_and_fusion.1), kind=kLoop, calls=%fused_computation.7 | loop fusion | flops 16777216 | bytes 50331680 | tf_op jit(solution)/shard_map/convert_element_type | solution.py:33
  33.2 12.1 %fusion.16 = (bf16[32,8,128,128]{3,1,2,0:T(8,128)(2,1)S(1)}, bf16[32,8,128,128]{3,1,2,0:T(8,128)(2,1)S(1)}) fusion(f32[2,32,8,16384]{3,2,0,1:T(8,128)} %convert_bitcast_fusion, f32[8,16384]{1,0:T(8,128)S(1)} %get-tuple-element.12, f32[8,16384]{1,0:T(8,128)S(1)} %get-tuple-element.11), kind=kLoop, calls=%fused_computation.18 | loop fusion | flops 33554432 | bytes 51380224
  45.3 7.7 %copy_bitcast_fusion = (bf16[1,32,8,128,128]{4,3,2,1,0:T(8,128)(2,1)}, bf16[1,32,8,128,128]{4,3,2,1,0:T(8,128)(2,1)}) fusion(bf16[32,8,128,128]{3,1,2,0:T(8,128)(2,1)S(1)} %get-tuple-element.10, bf16[32,8,128,128]{3,1,2,0:T(8,128)(2,1)S(1)} %get-tuple-element.9), kind=kLoop, calls=%fused_computation.20 | loop fusion | bytes 33554432 | tf_op jit(solution)/shard_map/stack | solution.py:37
  53.0 16.1 %fusion.3 = bf16[2,8,128,128,32]{2,3,0,4,1:T(8,128)(2,1)} fusion(bf16[1,128,2,128]{3,1,2,0:T(8,128)(2,1)S(1)} %get-tuple-element.16, bf16[1,128,2,128]{3,1,2,0:T(8,128)(2,1)S(1)} %get-tuple-element.15, bf16[1,32,8,128,128]{4,3,2,1,0:T(8,128)(2,1)} %get-tuple-element.19, bf16[1,32,8,128,128]{4,3,2,1,0:T(8,128)(2,1)} %get-tuple-element.20), kind=kOutput, calls=%fused_computation.10 | convolution fusion | flops 8615624704 | bytes 33685504 | tf_op jit(solution)/shard_map/okix,iaxbp->oakbp/dot_general | solution.py:43
  69.1 24.5 %copy.66 = bf16[2,8,128,128,32]{2,0,4,1,3:T(2,128)(2,1)} copy(bf16[2,8,128,128,32]{2,3,0,4,1:T(8,128)(2,1)} %fusion.3) | data formatting | bytes 33554432 | tf_op jit(solution)/shard_map/convert_element_type | solution.py:45
  93.7 7.6 %all-to-all-start = ((bf16[2,8,128,128,32]{2,0,4,1,3:T(2,128)(2,1)}), bf16[2,8,128,128,32]{2,0,4,1,3:T(2,128)(2,1)}, u32[]{:S(2)}, u32[]{:S(2)}) async-start(bf16[2,8,128,128,32]{2,0,4,1,3:T(2,128)(2,1)} %copy.66), calls=%async_computation | async-start | bytes 33554432 | tf_op jit(solution)/shard_map/all_to_all | solution.py:46
  102.1 0.5 broadcast.887
  102.6 0.7 fusion.52
  103.4 0.7 fusion.51
  104.2 0.7 gather_fusion.3
  105.1 293.0 %all-to-all-done = bf16[2,8,128,128,32]{2,0,4,1,3:T(2,128)(2,1)} async-done(((bf16[2,8,128,128,32]{2,0,4,1,3:T(2,128)(2,1)}), bf16[2,8,128,128,32]{2,0,4,1,3:T(2,128)(2,1)}, u32[]{:S(2)}, u32[]{:S(2)}) %all-to-all-start) | async-done | bytes 16777248 | tf_op jit(solution)/shard_map/all_to_all | solution.py:46
  398.1 33.1 %bitcast_convert_fusion = bf16[2,128,128,8,32]{2,1,4,3,0:T(8,128)(2,1)} fusion(bf16[2,8,128,16,8,32]{2,0,5,1,4,3:T(2,128)(2,1)} %bitcast.22, bf16[1,128,2,128]{3,1,2,0:T(8,128)(2,1)S(1)} %get-tuple-element.16, bf16[1,128,2,128]{3,1,2,0:T(8,128)(2,1)S(1)} %get-tuple-element.15), kind=kOutput, calls=%fused_computation.4 | convolution fusion | flops 4303618048 | bytes 33685504 | tf_op jit(solution)/shard_map/okix,ixabp->okabp/dot_general | solution.py:51
  431.2 46.6 %copy.68 = bf16[2,128,128,8,32]{4,3,2,1,0:T(8,128)(2,1)} copy(bf16[2,128,128,8,32]{2,1,4,3,0:T(8,128)(2,1)} %bitcast_convert_fusion) | data formatting | bytes 33554432 | tf_op jit(solution)/shard_map/convert_element_type | solution.py:53
  477.7 118.3 %copy.69 = bf16[2,131072,32]{2,0,1:T(2,128)(2,1)} copy(bf16[2,131072,32]{2,1,0:T(8,128)(2,1)} %bitcast.28) | data formatting | bytes 33554432 | tf_op jit(solution)/shard_map/reshape | solution.py:54
  596.1 2.4 gather_fusion.2
  598.6 0.6 copy.77
  599.3 3.3 all-to-all-start.1
  602.5 1.3 gather_fusion.1
  603.9 79.1 %all_gather.9 = bf16[2,2,4,8,32]{4,3,1,0,2:T(8,128)(2,1)S(1)} all-gather(bf16[2,2,1,8,32]{4,3,1,0,2:T(8,128)(2,1)S(1)} %copy_select_fusion), channel_id=1, replica_groups=mesh['pair'=2,'grow'=4,'gcol'=4] {'grow'}, dimensions={2}, use_global_device_ids=true | all-gather | bytes 10240 | tf_op jit(solution)/shard_map/all_gather | solution.py:78
  683.0 0.2 copy.71
  683.2 5.6 all_gather.10
  689.0 0.1 copy.73
  689.1 0.1 copy.72
  689.4 5.7 all_gather.11
  695.1 0.1 copy.80
  695.3 0.9 convolution_bitcast_fusion
  (35 shorter events, 1.1 us)
Async XLA Ops:
  0.0 104.2 %copy-start = (f32[64]{0:T(128)S(1)}, f32[64]{0:T(128)}, u32[]{:S(2)}) copy-start(f32[64]{0:T(128)} %param.10) | copy-start | bytes 772
  93.7 8.3 %copy-start.2 = (s32[3840]{0:T(1024)S(1)}, s32[3840]{0:T(1024)}, u32[]{:S(2)}) copy-start(s32[3840]{0:T(1024)} %param.12) | copy-start | bytes 46084
  93.7 9.7 %copy-start.3 = (s32[256]{0:T(256)S(1)}, s32[256]{0:T(256)}, u32[]{:S(2)}) copy-start(s32[256]{0:T(256)} %param.13) | copy-start | bytes 3076
  93.7 10.5 %copy-start.4 = (s32[1,32]{1,0:T(1,128)S(1)}, s32[1,32]{1,0:T(1,128)}, u32[]{:S(2)}) copy-start(s32[1,32]{1,0:T(1,128)} %param.9) | copy-start | bytes 388
  93.7 304.4 %all-to-all-start = ((bf16[2,8,128,128,32]{2,0,4,1,3:T(2,128)(2,1)}), bf16[2,8,128,128,32]{2,0,4,1,3:T(2,128)(2,1)}, u32[]{:S(2)}, u32[]{:S(2)}) async-start(bf16[2,8,128,128,32]{2,0,4,1,3:T(2,128)(2,1)} %copy.66), calls=%async_computation | async-start | bytes 33554432 | tf_op jit(solution)/shard_map/all_to_all | solution.py:46
  477.7 218.5 %copy-start.1 = (f32[64]{0:T(128)S(1)}, f32[64]{0:T(128)}, u32[]{:S(2)}) copy-start(f32[64]{0:T(128)} %param.10) | copy-start | bytes 772
  599.3 90.0 %all-to-all-start.1 = ((bf16[2,2,120,32]{2,3,0,1:T(8,128)(2,1)}), bf16[2,2,120,32]{2,3,0,1:T(8,128)(2,1)S(1)}, u32[]{:S(2)}, u32[]{:S(2)}) async-start(bf16[2,2,120,32]{2,3,0,1:T(8,128)(2,1)} %copy.77), calls=%async_computation.1 | async-start | bytes 65536 | tf_op jit(solution)/shard_map/all_to_all | solution.py:75
where the time goes:
time: 698 us; the launch traced here: 696 us
  waiting for transfers between devices  293 us (42%)
  local copies, waits for them, and re-layouts  217 us (31%)
  blocking collectives  90.5 us (13%)
  matrix products  50.2 us (7%)
  other arithmetic  33.7 us (5%)
  starting transfers between devices  10.8 us (2%)
    all_to_all x1, waiting for transfers between devices, on_device(): lax.all_to_all(second, ('grow', 'gcol'), split_axis=3, concat_axis=1, til...  293 us
    reshape x1, local copies, waits for them, and re-layouts, on_device(): flat = elements.reshape(2, -1, pairs_here)  118 us
    all_gather x1, blocking collectives, on_device(): lax.all_gather(cols.reshape(2, n_pair, 1, col_count, pairs_here), 'grow',...  79.1 us
    convert_element_type x1, local copies, waits for them, and re-layouts, on_device(): elements = jnp.einsum('okix,ixabp->okabp', table_first, moved, preferred_...  46.6 us
    dot_general x1, matrix products, on_device(): jnp.einsum('okix,ixabp->okabp', table_first, moved, preferred_element_typ...  33.1 us
    convert_element_type x1, local copies, waits for them, and re-layouts, on_device(): second = jnp.einsum('okix,iaxbp->oakbp', natural, third, preferred_elemen...  24.5 us
    convert_element_type x1, other arithmetic, on_device(): jnp.take(valence, pair_bands.reshape(-1), axis=1).astype(jnp.float32)  18.3 us
    dot_general x1, matrix products, on_device(): jnp.einsum('okix,iaxbp->oakbp', natural, third, preferred_element_type=jn...  16.1 us
  transfers between devices with their start and end apart: 2, of which 1 were waited for; matrix products, arithmetic and copies ran while one was open for 1% of the time, Pallas kernels for 0%

commit v1 on v0

--- a/solution.py
+++ b/solution.py
@@ -3,6 +3,8 @@
 import jax
 import jax.numpy as jnp
 from jax import lax
+from jax.experimental import pallas as pl
+from jax.experimental.pallas import tpu as pltpu
 from jax.sharding import PartitionSpec as P
 
 NGRID = 128
@@ -20,7 +22,7 @@
     return jnp.stack([upper, lower])
 
 
-def on_device(valence, conduction, pair_bands, e_val, e_cond, g_index, slab_index):
+def on_device_general(valence, conduction, pair_bands, e_val, e_cond, g_index, slab_index):
     n_pair = lax.axis_size("pair")
     n_grow = lax.axis_size("grow")
     n_gcol = lax.axis_size("gcol")
@@ -88,6 +90,176 @@
     )
 
 
+CHUNK = 16
+BLOCK_ROWS = 128
+
+
+def partial_kernel(bands, val, cond, t3, a2, pick, phase, spread, pack, out, vbuf, stage, third, sems):
+    pairs, planes = vbuf.shape[1], vbuf.shape[2]
+    lanes = pairs * planes
+    wide = CHUNK * NGRID
+    chunks = NGRID // CHUNK
+    for chunk in range(chunks):
+        at = pl.ds(chunk * wide, wide)
+
+        @pl.loop(0, pairs)
+        def _(pair):
+            pltpu.make_async_copy(
+                val.at[:, bands[pair], :, at], vbuf.at[:, pair, :, at], sems.at[chunk]
+            ).start()
+
+    @pl.loop(0, chunks)
+    def _(chunk):
+        at = pl.ds(pl.multiple_of(chunk * wide, wide), wide)
+        pltpu.make_async_copy(
+            vbuf.at[:, :, :, at], vbuf.at[:, :, :, at], sems.at[chunk]
+        ).wait()
+
+        @pl.loop(0, CHUNK)
+        def _(step):
+            here = pl.ds(pl.multiple_of(chunk * wide + step * NGRID, NGRID), NGRID)
+            c_re = cond[0, :, here].astype(jnp.float32)
+            c_im = cond[1, :, here].astype(jnp.float32)
+            reals, imags = [], []
+            for pair in range(pairs):
+                v_re = vbuf[0, pair, :, here].astype(jnp.float32)
+                v_im = vbuf[1, pair, :, here].astype(jnp.float32)
+                reals.append(v_re * c_re + v_im * c_im)
+                imags.append(v_re * c_im - v_im * c_re)
+            density = jnp.concatenate(
+                [jnp.concatenate(reals, axis=0), jnp.concatenate(imags, axis=0)], axis=1
+            ).astype(jnp.bfloat16)
+            moved = lax.dot_general(
+                t3[...], density, (((1,), (1,)), ((), ())), preferred_element_type=jnp.float32
+            )
+            for half in range(lanes // 128):
+                stage[half, pl.ds(step, 2 * NGRID, stride=CHUNK), :] = moved[
+                    :, half * 128 : (half + 1) * 128
+                ]
+
+        rows = pl.ds(pl.multiple_of(chunk * CHUNK, CHUNK), CHUNK)
+
+        @pl.loop(0, 2 * NGRID // 8)
+        def _(group):
+            for inner in range(8):
+                freq = group * 8 + inner
+                for half in range(lanes // 128):
+                    third[freq, rows, half * 128 : (half + 1) * 128] = stage[
+                        half, pl.ds(pl.multiple_of(freq * CHUNK, CHUNK), CHUNK), :
+                    ].astype(jnp.bfloat16)
+
+    blocks = pick.shape[0]
+    width = NGRID // blocks
+    ranges = a2.shape[0]
+    wide_two = NGRID // ranges
+
+    @pl.loop(0, blocks)
+    def _(block):
+        table = a2[block % ranges]
+        reals, imags = [], []
+        for inner in range(width):
+            freq = block * width + inner
+            field = jnp.concatenate([third[freq], third[NGRID + freq]], axis=0)
+            moved = jnp.dot(table, field, preferred_element_type=jnp.float32).astype(jnp.bfloat16)
+            reals.append(moved[:wide_two])
+            imags.append(moved[wide_two:])
+        chosen = pick[block]
+        re = jnp.dot(chosen, jnp.concatenate(reals, axis=0), preferred_element_type=jnp.float32)
+        im = jnp.dot(chosen, jnp.concatenate(imags, axis=0), preferred_element_type=jnp.float32)
+        both = jnp.dot(phase[block], spread[...], preferred_element_type=jnp.float32)
+        cosine, sine = both[:, :lanes], both[:, lanes:]
+        z_re = (cosine * re + sine * im).astype(jnp.bfloat16)
+        z_im = (cosine * im - sine * re).astype(jnp.bfloat16)
+        parts = []
+        for part in range(z_re.shape[0] // BLOCK_ROWS):
+            cut = slice(part * BLOCK_ROWS, (part + 1) * BLOCK_ROWS)
+            parts += [z_re[cut], z_im[cut]]
+        out[block] = jnp.dot(
+            jnp.concatenate(parts, axis=1), pack[...], preferred_element_type=jnp.float32
+        ).astype(out.dtype)
+
+
+def partial_sums(bands, valence, cond, t3, a2, pick, phase, spread, pack):
+    pairs, planes = bands.shape[0], valence.shape[2]
+    lanes = pairs * planes
+    blocks = pick.shape[0]
+    vmem = pl.BlockSpec(memory_space=pltpu.VMEM)
+    return pl.pallas_call(
+        partial_kernel,
+        out_shape=jax.ShapeDtypeStruct((blocks, BLOCK_ROWS, pack.shape[1]), jnp.bfloat16),
+        in_specs=[pl.BlockSpec(memory_space=pltpu.SMEM), pl.BlockSpec(memory_space=pl.ANY)] + [vmem] * 7,
+        out_specs=vmem,
+        scratch_shapes=[
+            pltpu.VMEM((2, pairs, planes, NGRID * NGRID), jnp.bfloat16),
+            pltpu.VMEM((lanes // 128, 2 * NGRID * CHUNK, 128), jnp.float32),
+            pltpu.VMEM((2 * NGRID, NGRID, lanes), jnp.bfloat16),
+            pltpu.SemaphoreType.DMA((NGRID // CHUNK,)),
+        ],
+        compiler_params=pltpu.CompilerParams(vmem_limit_bytes=58 * 2**20),
+        name="partial_sums",
+    )(bands, valence, cond, t3, a2, pick, phase, spread, pack)
+
+
+def prepare(valence, conduction, pair_bands, g_index, slab_index):
+    n_pair = lax.axis_size("pair")
+    n_grow = lax.axis_size("grow")
+    n_gcol = lax.axis_size("gcol")
+    blocks = n_grow * n_gcol
+    me = lax.axis_index("grow") * n_gcol + lax.axis_index("gcol")
+    planes = valence.shape[2]
+    pairs = pair_bands.size
+    lanes = pairs * planes
+    rows = g_index.reshape(n_pair, n_grow, n_gcol, -1).transpose(1, 2, 0, 3)
+    cols = slab_index.reshape(n_gcol, n_pair, n_grow, -1).transpose(2, 0, 1, 3)
+    points = jnp.concatenate([rows, cols], axis=3).reshape(blocks, -1)
+    wide_two = NGRID // n_gcol
+    spot = (points % planes) * wide_two + points // NGRID % wide_two
+    pick = (spot[:, :, None] == jnp.arange(planes * wide_two, dtype=jnp.int32)).astype(jnp.bfloat16)
+    first = points // (NGRID * NGRID)
+    where = me * planes + jnp.arange(planes, dtype=jnp.int32)
+    angle = (first[:, :, None] * where % NGRID).astype(jnp.float32) * (2.0 * math.pi / NGRID)
+    scale = 1.0 / math.sqrt(NGRID)
+    phase = jnp.concatenate([jnp.cos(angle) * scale, jnp.sin(angle) * scale], axis=2).astype(jnp.bfloat16)
+    lane = jnp.arange(2 * lanes, dtype=jnp.int32)
+    kind = lane // lanes * planes + lane % planes
+    spread = (jnp.arange(2 * planes, dtype=jnp.int32)[:, None] == kind).astype(jnp.bfloat16)
+    source = jnp.arange(2 * n_pair * lanes, dtype=jnp.int32)
+    target = source // lanes * pairs + source % lanes // planes
+    pack = (target[:, None] == jnp.arange(2 * n_pair * pairs, dtype=jnp.int32)).astype(jnp.bfloat16)
+    table = transform_table(NGRID, jnp.arange(NGRID, dtype=jnp.int32))
+    t3 = table.reshape(2 * NGRID, 2 * NGRID)
+    a2 = table.reshape(2, n_gcol, wide_two, 2 * NGRID).transpose(1, 0, 2, 3)
+    a2 = a2.reshape(n_gcol, 2 * wide_two, 2 * NGRID)
+    cond = conduction.reshape(2, planes, NGRID * NGRID)
+    return pair_bands.reshape(-1), valence, cond, t3, a2, pick, phase, spread, pack
+
+
+def on_device(valence, conduction, pair_bands, e_val, e_cond, g_index, slab_index):
+    if valence.shape[2] != 8 or pair_bands.size != 32:
+        return on_device_general(valence, conduction, pair_bands, e_val, e_cond, g_index, slab_index)
+    n_pair = lax.axis_size("pair")
+    n_grow = lax.axis_size("grow")
+    n_gcol = lax.axis_size("gcol")
+    pairs = pair_bands.size
+    sums = partial_sums(*prepare(valence, conduction, pair_bands, g_index, slab_index))
+    swapped = lax.all_to_all(sums, ("grow", "gcol"), split_axis=0, concat_axis=0, tiled=True)
+    elements = jnp.sum(swapped.astype(jnp.float32), axis=0).astype(jnp.bfloat16)
+    gaps = jnp.take(e_val, pair_bands) - e_cond[:, None]
+    weight = (2.0 / (gaps * math.sqrt(pairs * n_pair))).reshape(-1)
+    row_count = g_index.shape[0] // (n_pair * n_grow * n_gcol)
+    weighted = (elements[:row_count].astype(jnp.float32) * jnp.tile(weight, 2 * n_pair)).astype(jnp.bfloat16)
+    rows = lax.all_gather(weighted, ("pair", "gcol"), axis=0, tiled=False)
+    rows = rows.reshape(n_pair, n_gcol, row_count, n_pair, 2, pairs)
+    rows = lax.dynamic_index_in_dim(rows, lax.axis_index("pair"), axis=3, keepdims=False)
+    cols = lax.all_gather(elements[row_count:], ("pair", "grow"), axis=0, tiled=False)
+    cols = cols.reshape(n_pair, n_grow, -1, n_pair, 2, pairs)
+    conjugate = jnp.stack([jnp.stack([cols[..., 0, :], cols[..., 1, :]]), jnp.stack([-cols[..., 1, :], cols[..., 0, :]])])
+    result = jnp.einsum(
+        "scjik,oisgnpk->ocjpgn", rows, conjugate, preferred_element_type=jnp.float32
+    )
+    return result.reshape(2, n_gcol * row_count, -1)
+
+
 def solution(mesh):
     in_specs = (
         P(None, None, ("grow", "gcol"), None),

time: 698 us -> 131 us (0.19)
  waiting for transfers between devices: 293 us -> 13 us
  local copies, waits for them, and re-layouts: 217 us -> 7.06 us
  Pallas kernels: 0 us -> 61.1 us
  blocking collectives: 90.5 us -> 36.3 us
  matrix products: 50.2 us -> 0.23 us
  other arithmetic: 33.7 us -> 4.74 us
    all_to_all x2 -> x1, waiting for transfers between devices: 293 us -> 13 us  [on_device(): lax.all_to_all(sums, ('grow', 'gcol'), split_axis=0, concat_axis=0, tiled...]
    reshape x4 -> x6, local copies, waits for them, and re-layouts: 119 us -> 2.86 us  [the longest x1 0.87 us: on_device(): return result.reshape(2, n_gcol * row_count, -1)]
    convert_element_type x3 -> x0, local copies, waits for them, and re-layouts: 71.7 us -> none  [the longest x1 46.6 us: on_device(): elements = jnp.einsum('okix,ixabp->okabp', table_first, moved, preferred_...]
    pallas_call x0 -> x1, Pallas kernels: none -> 61.1 us  [partial_sums(): pl.pallas_call(partial_kernel, out_shape=jax.ShapeDtypeStruct((blocks, BL...]
    all_gather x3 -> x2, blocking collectives: 90.5 us -> 36.3 us  [the longest x1 27 us: on_device(): lax.all_gather(elements[row_count:], ('pair', 'grow'), axis=0, tiled=False)]
    dot_general x3 -> x1, matrix products: 50.2 us -> 0.23 us  [on_device(): jnp.einsum('scjik,oisgnpk->ocjpgn', rows, conjugate, preferred_element_ty...]
    convert_element_type x3 -> x4, other arithmetic: 19.5 us -> 3.24 us  [the longest x1 1.72 us: prepare(): (spot[:, :, None] == jnp.arange(planes * wide_two, dtype=jnp.int32)).asty...]
    gather x4 -> x0, local copies, waits for them, and re-layouts: 15.6 us -> none  [the longest x1 11.8 us: on_device(): jnp.take(valence, pair_bands.reshape(-1), axis=1).astype(jnp.float32)]
  transfers between devices with their start and end apart: 2 -> 1, of which waited for: 1 -> 1; matrix products, arithmetic and copies ran while one was open for 1% -> 1% of each run, Pallas kernels for 0% -> 0%
where the time goes in v1:
time: 131 us
  Pallas kernels  61.1 us (47%)
  blocking collectives  36.3 us (28%)
  waiting for transfers between devices  13 us (10%)
  starting transfers between devices  7.27 us (6%)
  local copies, waits for them, and re-layouts  7.06 us (5%)
  other arithmetic  4.74 us (4%)
    pallas_call x1, Pallas kernels, partial_sums(): pl.pallas_call(partial_kernel, out_shape=jax.ShapeDtypeStruct((blocks, BL...  61.1 us
    all_gather x1, blocking collectives, on_device(): lax.all_gather(elements[row_count:], ('pair', 'grow'), axis=0, tiled=False)  27 us
    all_to_all x1, waiting for transfers between devices, on_device(): lax.all_to_all(sums, ('grow', 'gcol'), split_axis=0, concat_axis=0, tiled...  13 us
    all_gather x1, blocking collectives, on_device(): rows = lax.all_gather(weighted, ('pair', 'gcol'), axis=0, tiled=False)  9.37 us
    all_to_all x1, starting transfers between devices, on_device(): lax.all_to_all(sums, ('grow', 'gcol'), split_axis=0, concat_axis=0, tiled...  7.27 us
  transfers between devices with their start and end apart: 1, of which 1 were waited for; matrix products, arithmetic and copies ran while one was open for 1% of the time, Pallas kernels for 0%

profile of v1, /device:TPU:0, one launch (start us, length us, event | category | flops | bytes accessed | tf_op | source)
XLA Modules:
  0.0 130.7 jit_solution(2020735425607222998)
XLA Ops:
  0.0 0.0 copy-start
  0.0 0.3 multiply_convert_fusion.2
  0.3 0.3 fusion.25
  0.6 0.8 reshape.300
  1.4 0.8 reshape.299
  2.2 0.1 pad_add_fusion
  2.3 0.6 multiply_convert_fusion.1
  3.0 1.3 %copy.44.phase = bf16[16,256,16]{2,1,0:T(8,128)(2,1)} copy(bf16[16,256,16]{1,2,0:T(8,128)(2,1)S(1)} %pad_maximum_fusion.1) | data formatting | bytes 262144 | tf_op jit(solution)/shard_map/concatenate | solution.py:222
  4.3 0.1 copy.39
  4.5 0.1 copy.40
  4.6 0.7 copy.41
  5.3 0.1 copy.38
  5.4 0.7 copy.73
  6.1 1.7 %fusion.pick = bf16[16,256,256]{2,1,0:T(8,128)(2,1)} fusion(s32[16,256]{1,0:T(8,128)S(1)} %get-tuple-element.20), kind=kLoop, calls=%fused_computation.2 | loop fusion | flops 2097152 | bytes 2113536 | tf_op jit(solution)/shard_map/convert_element_type | solution.py:217
  7.8 0.9 fusion.1.pack
  8.7 0.6 fusion.15.spread
  9.3 61.1 %partial_sums.1 = bf16[16,128,128]{2,1,0:T(8,128)(2,1)} custom-call(s32[32]{0:T(128)} %bitcast.88, bf16[2,64,8,16384]{3,2,1,0:T(8,128)(2,1)} %val.1, bf16[2,8,16384]{2,1,0:T(8,128)(2,1)} %bitcast.80, bf16[256,256]{1,0:T(8,128)(2,1)} %bitcast.82, bf16[4,64,256]{2,1,0:T(8,128)(2,1)} %bitcast.81, bf16[16,256,256]{2,1,0:T(8,128)(2,1)} %fusion.pick, ...), custom_call_target="tpu_custom_call" | custom-call | tf_op jit(solution)/shard_map/partial_sums/pallas_call | solution.py:187
  70.5 7.3 %all-to-all-start = ((bf16[16,128,128]{2,1,0:T(8,128)(2,1)}), bf16[16,128,128]{2,1,0:T(8,128)(2,1)S(1)}, u32[]{:S(2)}, u32[]{:S(2)}) async-start(bf16[16,128,128]{2,1,0:T(8,128)(2,1)} %partial_sums.1), calls=%async_computation | async-start | bytes 1048576 | tf_op jit(solution)/shard_map/all_to_all | solution.py:245
  78.4 0.7 gather_fusion
  79.2 0.1 mul.201
  79.2 13.0 %all-to-all-done = bf16[16,128,128]{2,1,0:T(8,128)(2,1)S(1)} async-done(((bf16[16,128,128]{2,1,0:T(8,128)(2,1)}), bf16[16,128,128]{2,1,0:T(8,128)(2,1)S(1)}, u32[]{:S(2)}, u32[]{:S(2)}) %all-to-all-start) | async-done | bytes 524320 | tf_op jit(solution)/shard_map/all_to_all | solution.py:245
  92.2 0.1 reduce_sum.12
  92.3 27.0 %all-gather = bf16[64,128]{1,0:T(8,128)(2,1)S(1)} all-gather(bf16[8,128]{1,0:T(8,128)(2,1)S(1)} %slice.20), channel_id=2, replica_groups=mesh['pair'=2,'grow'=4,'gcol'=4] {'pair','grow'}, dimensions={0}, use_global_device_ids=true | all-gather | bytes 18432 | tf_op jit(solution)/shard_map/all_gather | solution.py:254
  119.3 0.1 reshape.302
  119.4 0.1 fusion.55
  119.5 9.4 %all-gather.1 = bf16[960,128]{1,0:T(8,128)(2,1)S(1)} all-gather(bf16[120,128]{1,0:T(8,128)(2,1)S(1)} %multiply_convert_fusion.4), channel_id=3, replica_groups=mesh['pair'=2,'grow'=4,'gcol'=4] {'pair','gcol'}, dimensions={0}, use_global_device_ids=true | all-gather | bytes 276480 | tf_op jit(solution)/shard_map/all_gather | solution.py:251
  128.9 0.1 copy.47
  129.1 0.3 reshape.303
  129.4 0.1 constant_dynamic-slice_fusion
  129.5 0.2 convolution_bitcast_fusion
  129.7 0.1 copy.49
  129.8 0.9 reshape.304
  (24 shorter events, 0.3 us)
Async XLA Ops:
  0.0 78.4 %copy-start = (f32[64]{0:T(128)S(1)}, f32[64]{0:T(128)}, u32[]{:S(2)}) copy-start(f32[64]{0:T(128)} %param.10) | copy-start | bytes 772
  9.3 69.1 %copy-start.1 = (s32[1,32]{1,0:T(1,128)S(1)}, s32[1,32]{1,0:T(1,128)}, u32[]{:S(2)}) copy-start(s32[1,32]{1,0:T(1,128)} %param.9) | copy-start | bytes 388
  70.5 21.7 %all-to-all-start = ((bf16[16,128,128]{2,1,0:T(8,128)(2,1)}), bf16[16,128,128]{2,1,0:T(8,128)(2,1)S(1)}, u32[]{:S(2)}, u32[]{:S(2)}) async-start(bf16[16,128,128]{2,1,0:T(8,128)(2,1)} %partial_sums.1), calls=%async_computation | async-start | bytes 1048576 | tf_op jit(solution)/shard_map/all_to_all | solution.py:245

commit v2 on v0

--- a/solution.py
+++ b/solution.py
@@ -1,8 +1,12 @@
+import functools
 import math
 
 import jax
 import jax.numpy as jnp
+import numpy as np
 from jax import lax
+from jax.experimental import pallas as pl
+from jax.experimental.pallas import tpu as pltpu
 from jax.sharding import PartitionSpec as P
 
 NGRID = 128
@@ -20,7 +24,7 @@
     return jnp.stack([upper, lower])
 
 
-def on_device(valence, conduction, pair_bands, e_val, e_cond, g_index, slab_index):
+def on_device_general(valence, conduction, pair_bands, e_val, e_cond, g_index, slab_index):
     n_pair = lax.axis_size("pair")
     n_grow = lax.axis_size("grow")
     n_gcol = lax.axis_size("gcol")
@@ -88,6 +92,336 @@
     )
 
 
+CHUNK = 16
+PITCH = 17
+SLOTS = 3
+BLOCK_ROWS = 128
+MESH = pl.DeviceIdType.MESH
+
+
+def slab_kernel(
+    sizes, row_count, bands, e_val, e_cond, val, cond, points, t3, out,
+    slot_a, slot_b, slot_c, stage, third, pack, spread, sums, inbox, row_out, row_in, col_out, col_in,
+    sems, sum_send, sum_recv, row_send, row_recv, col_send, col_recv,
+):
+    n_pair, n_grow, n_gcol = sizes
+    blocks = n_grow * n_gcol
+    pair_at = lax.axis_index("pair")
+    grow_at = lax.axis_index("grow")
+    gcol_at = lax.axis_index("gcol")
+    me = grow_at * n_gcol + gcol_at
+    half = BLOCK_ROWS // 2
+    col_count = BLOCK_ROWS - row_count
+    pairs = bands.shape[0]
+    held = (slot_a, slot_b, slot_c)
+    slots = len(held)
+    planes, wide = slot_a.shape[2], slot_a.shape[3]
+    lanes = pairs * planes
+    chunks = NGRID // CHUNK
+
+    def place(pair, grow, gcol):
+        return {"pair": pair, "grow": grow, "gcol": gcol}
+
+    def arrival(src, dst, send, recv):
+        at = place(lax.rem(pair_at + 1, n_pair), grow_at, gcol_at)
+        return pltpu.make_async_remote_copy(
+            src_ref=src, dst_ref=dst, send_sem=send, recv_sem=recv, device_id=at, device_id_type=MESH
+        )
+
+    def block_place(distance):
+        other = lax.rem(me + distance, blocks)
+        return other, place(pair_at, other // n_gcol, lax.rem(other, n_gcol))
+
+    def fetch(chunk):
+        return pltpu.make_async_copy(
+            val.at[:, :, :, pl.ds(chunk * wide, wide)], held[chunk % slots], sems.at[chunk % slots]
+        )
+
+    for chunk in range(slots - 1):
+        fetch(chunk).start()
+
+    barrier = pltpu.get_barrier_semaphore()
+    greeted = 0
+    for distance in range(1, blocks):
+        pl.semaphore_signal(barrier, inc=1, device_id=block_place(distance)[1], device_id_type=MESH)
+        greeted += 1
+    for far in range(1, n_pair):
+        other = lax.rem(pair_at + far, n_pair)
+        for step in range(n_gcol):
+            at = place(other, grow_at, lax.rem(gcol_at + step, n_gcol))
+            pl.semaphore_signal(barrier, inc=1, device_id=at, device_id_type=MESH)
+            greeted += 1
+        for step in range(1, n_grow):
+            at = place(other, lax.rem(grow_at + step, n_grow), gcol_at)
+            pl.semaphore_signal(barrier, inc=1, device_id=at, device_id_type=MESH)
+            greeted += 1
+
+    source = lax.broadcasted_iota(jnp.int32, pack.shape, 0)
+    target = source // lanes * pairs + source % lanes // planes
+    pack[...] = jnp.where(
+        target == lax.broadcasted_iota(jnp.int32, pack.shape, 1), 1.0, 0.0
+    ).astype(jnp.bfloat16)
+    plane = lax.broadcasted_iota(jnp.int32, (NGRID, lanes), 1) % planes + me * planes
+    expand = jnp.where(
+        lax.broadcasted_iota(jnp.int32, (NGRID, lanes), 0) == plane, 1.0, 0.0
+    ).astype(jnp.bfloat16)
+    for part in range(2):
+        spread[:, part * lanes : (part + 1) * lanes] = jnp.dot(
+            t3[:NGRID, part * NGRID : (part + 1) * NGRID], expand, preferred_element_type=jnp.float32
+        ).astype(jnp.bfloat16)
+    spot_of = lax.broadcasted_iota(jnp.int32, (1, 4 * pairs), 1) % pairs
+    energy = jnp.zeros((1, 4 * pairs), jnp.float32)
+    for pair in range(pairs):
+        energy = jnp.where(spot_of == pair, e_val[bands[pair]], energy)
+    weight = 2.0 / ((energy - e_cond[0]) * math.sqrt(pairs * n_pair))
+
+    for chunk in range(chunks):
+        slot = held[chunk % slots]
+        fetch(chunk).wait()
+        if chunk + slots - 1 < chunks:
+            fetch(chunk + slots - 1).start()
+
+        @pl.loop(0, CHUNK, unroll=4)
+        def _(step):
+            there = pl.ds(pl.multiple_of(chunk * wide + step * NGRID, NGRID), NGRID)
+            here = pl.ds(pl.multiple_of(step * NGRID, NGRID), NGRID)
+            c_re = cond[0, 0, :, there].astype(jnp.float32)
+            c_im = cond[1, 0, :, there].astype(jnp.float32)
+            reals, imags = [], []
+            for pair in range(pairs):
+                v_re = slot[0, bands[pair], :, here].astype(jnp.float32)
+                v_im = slot[1, bands[pair], :, here].astype(jnp.float32)
+                reals.append(v_re * c_re + v_im * c_im)
+                imags.append(v_re * c_im - v_im * c_re)
+            density = jnp.concatenate(
+                [jnp.concatenate(reals, axis=0), jnp.concatenate(imags, axis=0)], axis=1
+            ).astype(jnp.bfloat16)
+            moved = lax.dot_general(
+                t3[...], density, (((1,), (1,)), ((), ())), preferred_element_type=jnp.float32
+            )
+            for part in range(lanes // 128):
+                stage[part, pl.ds(step, 2 * NGRID, stride=PITCH), :] = moved[
+                    :, part * 128 : (part + 1) * 128
+                ]
+
+        rows = pl.ds(chunk * CHUNK, CHUNK)
+
+        @pl.loop(0, 2 * NGRID // 8)
+        def _(group):
+            for inner in range(8):
+                freq = group * 8 + inner
+                start = pl.multiple_of(group * (8 * PITCH), 8) + inner * PITCH
+                for part in range(lanes // 128):
+                    third[freq, rows, part * 128 : (part + 1) * 128] = stage[
+                        part, pl.ds(start, CHUNK), :
+                    ].astype(jnp.bfloat16)
+
+    width = NGRID // blocks
+    wide_two = NGRID // n_gcol
+    count = points.shape[1]
+
+    def partial_sums(block):
+        first_row = pl.multiple_of(lax.rem(block, n_gcol) * wide_two, wide_two)
+        table = jnp.concatenate(
+            [t3[pl.ds(first_row, wide_two), :], t3[pl.ds(first_row + NGRID, wide_two), :]], axis=0
+        )
+        reals, imags = [], []
+        for inner in range(width):
+            freq = block * width + inner
+            field = jnp.concatenate([third[freq], third[NGRID + freq]], axis=0)
+            moved = jnp.dot(table, field, preferred_element_type=jnp.float32).astype(jnp.bfloat16)
+            reals.append(moved[:wide_two])
+            imags.append(moved[wide_two:])
+        listed = points[pl.ds(block, 1), :]
+        spot = (listed & (width - 1)) * wide_two + ((listed >> 7) & (wide_two - 1))
+        chosen = jnp.where(
+            lax.broadcasted_iota(jnp.int32, (width * wide_two, count), 0) == spot, 1.0, 0.0
+        ).astype(jnp.bfloat16)
+        wave = jnp.where(
+            lax.broadcasted_iota(jnp.int32, (NGRID, count), 0) == (listed >> 14), 1.0, 0.0
+        ).astype(jnp.bfloat16)
+
+        def choose(mask, field):
+            return lax.dot_general(
+                mask, field, (((0,), (0,)), ((), ())), preferred_element_type=jnp.float32
+            )
+
+        re = choose(chosen, jnp.concatenate(reals, axis=0))
+        im = choose(chosen, jnp.concatenate(imags, axis=0))
+        both = choose(wave, spread[...])
+        cosine, sine = both[:, :lanes], both[:, lanes:]
+        z_re = (cosine * re + sine * im).astype(jnp.bfloat16)
+        z_im = (cosine * im - sine * re).astype(jnp.bfloat16)
+        parts = []
+        for low in range(0, BLOCK_ROWS, half):
+            for z in (z_re, z_im):
+                starts = range(low, count, BLOCK_ROWS)
+                parts.append(jnp.concatenate([z[at : at + half] for at in starts], axis=0))
+        return jnp.dot(
+            jnp.concatenate(parts, axis=1), pack[...], preferred_element_type=jnp.float32
+        )
+
+    def sum_copy(distance):
+        other, at = block_place(distance)
+        return pltpu.make_async_remote_copy(
+            src_ref=sums.at[distance], dst_ref=inbox.at[distance],
+            send_sem=sum_send.at[distance], recv_sem=sum_recv.at[distance],
+            device_id=at, device_id_type=MESH,
+        )
+
+    pl.semaphore_wait(barrier, greeted)
+
+    @pl.loop(1, blocks, unroll=3)
+    def _(distance):
+        sums[distance] = partial_sums(lax.rem(me + distance, blocks)).astype(jnp.bfloat16)
+        sum_copy(distance).start()
+
+    total = partial_sums(me)
+    for distance in range(1, blocks):
+        sum_copy(distance).wait_recv()
+        total = total + inbox[distance].astype(jnp.float32)
+    elements = total.astype(jnp.bfloat16).astype(jnp.float32)
+    weighted = (elements * weight).astype(jnp.bfloat16)
+    cols = [elements[(one + 1) * half - col_count : (one + 1) * half] for one in range(n_pair)]
+    cols = jnp.concatenate(cols, axis=0).astype(jnp.bfloat16)
+    col_out[...] = cols
+    for one in range(n_pair):
+        row_out[one] = weighted[one * half : (one + 1) * half]
+    row_slot = pair_at * n_gcol + gcol_at
+    col_slot = pair_at * n_grow + grow_at
+    row_copies, col_copies = [], []
+    for far in range(n_pair):
+        other = lax.rem(pair_at + far, n_pair)
+        behind = lax.rem(pair_at + n_pair - far, n_pair)
+        for step in range(n_grow):
+            if far or step:
+                number = far * n_grow + step
+                copy = pltpu.make_async_remote_copy(
+                    src_ref=col_out, dst_ref=col_in.at[col_slot],
+                    send_sem=col_send.at[number], recv_sem=col_recv.at[col_slot],
+                    device_id=place(other, lax.rem(grow_at + step, n_grow), gcol_at),
+                    device_id_type=MESH,
+                )
+                copy.start()
+                source = behind * n_grow + lax.rem(grow_at + n_grow - step, n_grow)
+                col_copies.append((copy, source))
+        for step in range(n_gcol):
+            if far or step:
+                number = far * n_gcol + step
+                copy = pltpu.make_async_remote_copy(
+                    src_ref=row_out.at[other], dst_ref=row_in.at[row_slot],
+                    send_sem=row_send.at[number], recv_sem=row_recv.at[row_slot],
+                    device_id=place(other, grow_at, lax.rem(gcol_at + step, n_gcol)),
+                    device_id_type=MESH,
+                )
+                copy.start()
+                source = behind * n_gcol + lax.rem(gcol_at + n_gcol - step, n_gcol)
+                row_copies.append((copy, source))
+    col_in[col_slot] = cols
+    row_in[row_slot] = row_out[pair_at]
+    for _, source in col_copies:
+        arrival(col_out, col_in.at[source], col_send.at[0], col_recv.at[source]).wait_recv()
+    lane = lax.broadcasted_iota(jnp.int32, (out.shape[2], 4 * pairs), 1)
+    tables = {}
+    for one in range(n_pair):
+        pieces = []
+        for target in range(n_pair):
+            for grow in range(n_grow):
+                piece = col_in[one * n_grow + grow].astype(jnp.float32)
+                pieces.append(piece[target * col_count : (target + 1) * col_count])
+        straight = jnp.where(lane >= 2 * pairs, jnp.concatenate(pieces, axis=0), 0.0)
+        crossed = jnp.where(
+            lane >= 3 * pairs,
+            pltpu.roll(straight, pairs, 1),
+            jnp.where(lane >= 2 * pairs, -pltpu.roll(straight, 3 * pairs, 1), 0.0),
+        )
+        for part, table in enumerate((straight, crossed)):
+            tables[one, 1, part] = table.astype(jnp.bfloat16)
+            tables[one, 0, part] = pltpu.roll(table, 2 * pairs, 1).astype(jnp.bfloat16)
+    for _, source in row_copies:
+        arrival(row_out.at[0], row_in.at[source], row_send.at[0], row_recv.at[source]).wait_recv()
+    rows = [
+        jnp.concatenate([row_in[one * n_gcol + gcol] for gcol in range(n_gcol)], axis=0)
+        for one in range(n_pair)
+    ]
+    rows = jnp.concatenate(rows, axis=1)
+    for low in range(2):
+        for part in range(2):
+            table = jnp.concatenate([tables[one, low, part] for one in range(n_pair)], axis=1)
+            made = lax.dot_general(
+                rows, table, (((1,), (1,)), ((), ())), preferred_element_type=jnp.float32
+            )
+            kept = min(half, row_count - low * half)
+            for gcol in range(n_gcol):
+                start = gcol * row_count + low * half
+                out[part, start : start + kept, :] = made[gcol * half : gcol * half + kept]
+    for distance in range(1, blocks):
+        sum_copy(distance).wait_send()
+    for copy, _ in col_copies + row_copies:
+        copy.wait_send()
+
+
+def fixed_table():
+    freq = np.arange(NGRID, dtype=np.int32)
+    angle = (freq[:, None] * freq[None, :] % NGRID).astype(np.float32) * np.float32(2.0 * math.pi / NGRID)
+    scale = np.float32(1.0 / math.sqrt(NGRID))
+    cosine = np.cos(angle) * scale
+    sine = np.sin(angle) * scale
+    return np.block([[cosine, sine], [-sine, cosine]]).astype(jnp.bfloat16)
+
+
+def on_device(valence, conduction, pair_bands, e_val, e_cond, g_index, slab_index):
+    n_pair = lax.axis_size("pair")
+    n_grow = lax.axis_size("grow")
+    n_gcol = lax.axis_size("gcol")
+    blocks = n_grow * n_gcol
+    _, bands_all, planes, merged = valence.shape
+    pairs = pair_bands.size
+    row_count = g_index.size // (n_pair * blocks)
+    col_count = slab_index.size // (n_pair * blocks)
+    if (planes, pairs, n_pair, pair_bands.shape[0], row_count + col_count) != (8, 32, 2, 1, BLOCK_ROWS):
+        return on_device_general(valence, conduction, pair_bands, e_val, e_cond, g_index, slab_index)
+    rows = g_index.reshape(n_pair, n_grow, n_gcol, -1).transpose(1, 2, 0, 3)
+    cols = slab_index.reshape(n_gcol, n_pair, n_grow, -1).transpose(2, 0, 1, 3)
+    points = jnp.concatenate([rows, cols], axis=3).reshape(blocks, -1)
+    lanes = pairs * planes
+    half = BLOCK_ROWS // 2
+    width = 4 * pairs
+    vmem = pl.BlockSpec(memory_space=pltpu.VMEM)
+    smem = pl.BlockSpec(memory_space=pltpu.SMEM)
+    sem = pltpu.SemaphoreType.DMA
+    bf16 = jnp.bfloat16
+    return pl.pallas_call(
+        functools.partial(slab_kernel, (n_pair, n_grow, n_gcol), row_count),
+        out_shape=jax.ShapeDtypeStruct(
+            (2, n_gcol * row_count, n_pair * n_grow * col_count), jnp.float32
+        ),
+        in_specs=[smem, smem, smem, pl.BlockSpec(memory_space=pl.ANY), vmem, vmem, vmem],
+        out_specs=vmem,
+        scratch_shapes=[
+            *[pltpu.VMEM((2, bands_all, planes, CHUNK * NGRID), bf16)] * SLOTS,
+            pltpu.VMEM((lanes // 128, 2 * NGRID * PITCH, 128), jnp.float32),
+            pltpu.VMEM((2 * NGRID, NGRID, lanes), bf16),
+            pltpu.VMEM((4 * lanes, width), bf16),
+            pltpu.VMEM((NGRID, 2 * lanes), bf16),
+            pltpu.VMEM((blocks, BLOCK_ROWS, width), bf16),
+            pltpu.VMEM((blocks, BLOCK_ROWS, width), bf16),
+            pltpu.VMEM((n_pair, half, width), bf16),
+            pltpu.VMEM((n_pair * n_gcol, half, width), bf16),
+            pltpu.VMEM((n_pair * col_count, width), bf16),
+            pltpu.VMEM((n_pair * n_grow, n_pair * col_count, width), bf16),
+            sem((SLOTS,)),
+            sem((blocks,)), sem((blocks,)),
+            sem((n_pair * n_gcol,)), sem((n_pair * n_gcol,)),
+            sem((n_pair * n_grow,)), sem((n_pair * n_grow,)),
+        ],
+        compiler_params=pltpu.CompilerParams(
+            collective_id=0, has_side_effects=True, vmem_limit_bytes=52 * 2**20
+        ),
+        name="slab",
+    )(pair_bands.reshape(-1), e_val, e_cond, valence, conduction, points, jnp.asarray(fixed_table()))
+
+
 def solution(mesh):
     in_specs = (
         P(None, None, ("grow", "gcol"), None),

time: 698 us -> 48 us (0.07)
  waiting for transfers between devices: 293 us -> 0 us
  local copies, waits for them, and re-layouts: 217 us -> 5.74 us
  blocking collectives: 90.5 us -> 0 us
  matrix products: 50.2 us -> 0 us
  Pallas kernels: 0 us -> 41.2 us
  other arithmetic: 33.7 us -> 0.08 us
  starting transfers between devices: 10.8 us -> 0 us
    all_to_all x2 -> x0, waiting for transfers between devices: 293 us -> none  [the longest x1 293 us: on_device(): lax.all_to_all(second, ('grow', 'gcol'), split_axis=3, concat_axis=1, til...]
    reshape x4 -> x3, local copies, waits for them, and re-layouts: 119 us -> 1.58 us  [the longest x1 0.81 us: on_device(): rows = g_index.reshape(n_pair, n_grow, n_gcol, -1).transpose(1, 2, 0, 3)]
    all_gather x3 -> x0, blocking collectives: 90.5 us -> none  [the longest x1 79.1 us: on_device(): lax.all_gather(cols.reshape(2, n_pair, 1, col_count, pairs_here), 'grow',...]
    convert_element_type x3 -> x0, local copies, waits for them, and re-layouts: 71.7 us -> none  [the longest x1 46.6 us: on_device(): elements = jnp.einsum('okix,ixabp->okabp', table_first, moved, preferred_...]
    dot_general x3 -> x0, matrix products: 50.2 us -> none  [the longest x1 33.1 us: on_device(): jnp.einsum('okix,ixabp->okabp', table_first, moved, preferred_element_typ...]
    pallas_call x0 -> x1, Pallas kernels: none -> 41.2 us  [on_device(): pl.pallas_call(functools.partial(slab_kernel, (n_pair, n_grow, n_gcol), r...]
    convert_element_type x4 -> x0, other arithmetic: 19.8 us -> none  [the longest x1 18.3 us: on_device(): jnp.take(valence, pair_bands.reshape(-1), axis=1).astype(jnp.float32)]
    gather x5 -> x0, local copies, waits for them, and re-layouts: 16.3 us -> none  [the longest x1 11.8 us: on_device(): jnp.take(valence, pair_bands.reshape(-1), axis=1).astype(jnp.float32)]
  transfers between devices with their start and end apart: 2 -> 0, of which waited for: 1 -> 0; matrix products, arithmetic and copies ran while one was open for 1% -> 0% of each run, Pallas kernels for 0% -> 0%
where the time goes in v2:
time: 48 us; the launch traced here: 47.8 us
  Pallas kernels  41.2 us (86%)
  local copies, waits for them, and re-layouts  5.74 us (12%)
  between operations  0.7 us (1%)
    pallas_call x1, Pallas kernels, on_device(): pl.pallas_call(functools.partial(slab_kernel, (n_pair, n_grow, n_gcol), r...  41.2 us
    unnamed x9, local copies, waits for them, and re-layouts  3.25 us

profile of v2, /device:TPU:0, one launch (start us, length us, event | category | flops | bytes accessed | tf_op | source)
XLA Modules:
  0.0 47.8 jit_solution(11540057975470141782)
XLA Ops:
  0.7 0.8 %reshape.13 = s32[2,4,4,120]{3,2,1,0:T(4,128)S(1)} reshape(s32[3840]{0:T(1024)} %param.13) | data formatting | bytes 30720 | tf_op jit(solution)/shard_map/reshape | solution.py:384
  1.5 0.8 %reshape.14 = s32[4,2,4,8]{3,2,1,0:T(4,128)S(1)} reshape(s32[256]{0:T(256)} %param.14) | data formatting | bytes 2048 | tf_op jit(solution)/shard_map/reshape | solution.py:385
  2.3 0.1 pad_add_fusion
  2.4 0.0 copy-start
  2.4 1.0 %copy-done = bf16[2,1,8,16384]{3,2,1,0:T(8,128)(2,1)S(1)} copy-done((bf16[2,1,8,16384]{3,2,1,0:T(8,128)(2,1)S(1)}, bf16[2,1,8,16384]{3,2,1,0:T(8,128)(2,1)}, u32[]{:S(2)}) %copy-start) | copy-done | bytes 524312
  3.4 0.0 copy-start.1
  3.4 0.9 %copy-done.1 = bf16[256,256]{1,0:T(8,128)(2,1)S(1)} copy-done((bf16[256,256]{1,0:T(8,128)(2,1)S(1)}, bf16[256,256]{1,0:T(8,128)(2,1)}, u32[]{:S(2)}) %copy-start.1) | copy-done | bytes 131096
  4.3 0.0 copy-start.2
  4.3 0.7 %copy-done.2 = s32[1,32]{1,0:T(1,128)S(1)} copy-done((s32[1,32]{1,0:T(1,128)S(1)}, s32[1,32]{1,0:T(1,128)}, u32[]{:S(2)}) %copy-start.2) | copy-done | bytes 152
  5.0 0.0 copy-start.3
  5.0 0.7 %copy-done.3 = f32[64]{0:T(128)S(1)} copy-done((f32[64]{0:T(128)S(1)}, f32[64]{0:T(128)}, u32[]{:S(2)}) %copy-start.3) | copy-done | bytes 280
  5.6 41.2 %slab.1 = f32[2,480,64]{2,1,0:T(8,128)S(1)} custom-call(s32[32]{0:T(128)S(1)} %bitcast.11, f32[64]{0:T(128)S(1)} %copy-done.3, f32[1]{0:T(128)S(6)} %copy.18.e_cond, bf16[2,64,8,16384]{3,2,1,0:T(8,128)(2,1)} %val.1, bf16[2,1,8,16384]{3,2,1,0:T(8,128)(2,1)S(1)} %copy-done, s32[16,256]{1,0:T(8,128)S(1)} %bitcast.10, bf16[256,256]{1,0:T(8,128)(2,1)S(1)} %copy-done.1), custom_call_target="tpu_custom_call" | custom-call | tf_op jit(solution)/shard_map/slab/pallas_call | solution.py:394
  46.9 0.9 %copy.12 = f32[2,480,64]{1,2,0:T(8,128)} copy(f32[2,480,64]{2,1,0:T(8,128)S(1)} %slab.1) | data formatting | bytes 491520 | tf_op jit(solution)/shard_map/slab/pallas_call | solution.py:394
  (3 shorter events, 0.0 us)
Async XLA Ops:
  2.4 1.0 %copy-start = (bf16[2,1,8,16384]{3,2,1,0:T(8,128)(2,1)S(1)}, bf16[2,1,8,16384]{3,2,1,0:T(8,128)(2,1)}, u32[]{:S(2)}) copy-start(bf16[2,1,8,16384]{3,2,1,0:T(8,128)(2,1)} %cond.1) | copy-start | bytes 1572868
  3.4 0.9 %copy-start.1 = (bf16[256,256]{1,0:T(8,128)(2,1)S(1)}, bf16[256,256]{1,0:T(8,128)(2,1)}, u32[]{:S(2)}) copy-start(bf16[256,256]{1,0:T(8,128)(2,1)} %constant.2.clone.t3) | copy-start | bytes 393220
  4.3 0.7 %copy-start.2 = (s32[1,32]{1,0:T(1,128)S(1)}, s32[1,32]{1,0:T(1,128)}, u32[]{:S(2)}) copy-start(s32[1,32]{1,0:T(1,128)} %param.10) | copy-start | bytes 388
  5.0 0.7 %copy-start.3 = (f32[64]{0:T(128)S(1)}, f32[64]{0:T(128)}, u32[]{:S(2)}) copy-start(f32[64]{0:T(128)} %e_val.1) | copy-start | bytes 772

commit v3 on v2

--- a/solution.py
+++ b/solution.py
@@ -100,9 +100,10 @@
 
 
 def slab_kernel(
-    sizes, row_count, bands, e_val, e_cond, val, cond, points, t3, out,
-    slot_a, slot_b, slot_c, stage, third, pack, spread, sums, inbox, row_out, row_in, col_out, col_in,
-    sems, sum_send, sum_recv, row_send, row_recv, col_send, col_recv,
+    sizes, row_count, bands_in, e_val_in, e_cond, val, cond_in, g_rows_in, slab_rows_in, t3_in, out,
+    bands, e_val, cond, g_rows, slab_rows, t3,
+    slot_a, slot_b, slot_c, stage_a, stage_b, third, pack, spread, sums, inbox, row_out, row_in, col_out, col_in,
+    sems, load_sems, sum_send, sum_recv, row_send, row_recv, col_send, col_recv,
 ):
     n_pair, n_grow, n_gcol = sizes
     blocks = n_grow * n_gcol
@@ -112,7 +113,8 @@
     me = grow_at * n_gcol + gcol_at
     half = BLOCK_ROWS // 2
     col_count = BLOCK_ROWS - row_count
-    pairs = bands.shape[0]
+    pairs = bands.shape[1]
+    stages = (stage_a, stage_b)
     held = (slot_a, slot_b, slot_c)
     slots = len(held)
     planes, wide = slot_a.shape[2], slot_a.shape[3]
@@ -137,6 +139,14 @@
             val.at[:, :, :, pl.ds(chunk * wide, wide)], held[chunk % slots], sems.at[chunk % slots]
         )
 
+    loads = [
+        pltpu.make_async_copy(src, dst, load_sems.at[number])
+        for number, (src, dst) in enumerate(
+            ((bands_in, bands), (e_val_in, e_val), (t3_in, t3), (cond_in, cond), (g_rows_in, g_rows), (slab_rows_in, slab_rows))
+        )
+    ]
+    for load in loads:
+        load.start()
     for chunk in range(slots - 1):
         fetch(chunk).start()
 
@@ -156,6 +166,8 @@
             pl.semaphore_signal(barrier, inc=1, device_id=at, device_id_type=MESH)
             greeted += 1
 
+    for load in loads:
+        load.wait()
     source = lax.broadcasted_iota(jnp.int32, pack.shape, 0)
     target = source // lanes * pairs + source % lanes // planes
     pack[...] = jnp.where(
@@ -172,8 +184,18 @@
     spot_of = lax.broadcasted_iota(jnp.int32, (1, 4 * pairs), 1) % pairs
     energy = jnp.zeros((1, 4 * pairs), jnp.float32)
     for pair in range(pairs):
-        energy = jnp.where(spot_of == pair, e_val[bands[pair]], energy)
+        energy = jnp.where(spot_of == pair, e_val[bands[0, pair]], energy)
     weight = 2.0 / ((energy - e_cond[0]) * math.sqrt(pairs * n_pair))
+
+    groups = 2 * NGRID // 8 // CHUNK
+
+    def settle(chunk, group):
+        for inner in range(8):
+            start = pl.multiple_of(group * (8 * PITCH), 8) + inner * PITCH
+            for part in range(lanes // 128):
+                third[group * 8 + inner, chunk * CHUNK : (chunk + 1) * CHUNK, part * 128 : (part + 1) * 128] = (
+                    stages[chunk % 2][part, pl.ds(start, CHUNK), :].astype(jnp.bfloat16)
+                )
 
     for chunk in range(chunks):
         slot = held[chunk % slots]
@@ -189,8 +211,8 @@
             c_im = cond[1, 0, :, there].astype(jnp.float32)
             reals, imags = [], []
             for pair in range(pairs):
-                v_re = slot[0, bands[pair], :, here].astype(jnp.float32)
-                v_im = slot[1, bands[pair], :, here].astype(jnp.float32)
+                v_re = slot[0, bands[0, pair], :, here].astype(jnp.float32)
+                v_im = slot[1, bands[0, pair], :, here].astype(jnp.float32)
                 reals.append(v_re * c_re + v_im * c_im)
                 imags.append(v_re * c_im - v_im * c_re)
             density = jnp.concatenate(
@@ -200,25 +222,41 @@
                 t3[...], density, (((1,), (1,)), ((), ())), preferred_element_type=jnp.float32
             )
             for part in range(lanes // 128):
-                stage[part, pl.ds(step, 2 * NGRID, stride=PITCH), :] = moved[
+                stages[chunk % 2][part, pl.ds(step, 2 * NGRID, stride=PITCH), :] = moved[
                     :, part * 128 : (part + 1) * 128
                 ]
 
-        rows = pl.ds(chunk * CHUNK, CHUNK)
-
-        @pl.loop(0, 2 * NGRID // 8)
-        def _(group):
-            for inner in range(8):
-                freq = group * 8 + inner
-                start = pl.multiple_of(group * (8 * PITCH), 8) + inner * PITCH
-                for part in range(lanes // 128):
-                    third[freq, rows, part * 128 : (part + 1) * 128] = stage[
-                        part, pl.ds(start, CHUNK), :
-                    ].astype(jnp.bfloat16)
+            if chunk:
+                for group in range(groups):
+                    settle(chunk - 1, step * groups + group)
+
+    @pl.loop(0, 2 * NGRID // 8)
+    def _(group):
+        settle(chunks - 1, group)
 
     width = NGRID // blocks
     wide_two = NGRID // n_gcol
-    count = points.shape[1]
+    count = n_pair * BLOCK_ROWS
+    across = lax.broadcasted_iota(jnp.int32, (1, BLOCK_ROWS), 1)
+
+    def listed_points(block):
+        grow, gcol = block // n_gcol, lax.rem(block, n_gcol)
+        found = []
+        for pair in range(n_pair):
+            start = ((pair * n_grow + grow) * n_gcol + gcol) * row_count
+            line, offset = start // 128, lax.rem(start, 128)
+            back = lax.rem(128 - offset, 128)
+            split = 128 - offset
+            here = pltpu.roll(g_rows[pl.ds(line, 1), :], back, 1)
+            after = pltpu.roll(g_rows[pl.ds(lax.rem(line + 1, g_rows.shape[0]), 1), :], back, 1)
+            start = ((gcol * n_pair + pair) * n_grow + grow) * col_count
+            line, offset = start // 128, lax.rem(start, 128)
+            cols = pltpu.roll(
+                slab_rows[pl.ds(line, 1), :], lax.rem(row_count + 128 - offset, 128), 1
+            )
+            rows = jnp.where(across < split, here, after)
+            found.append(jnp.where(across < row_count, rows, cols))
+        return jnp.concatenate(found, axis=1)
 
     def partial_sums(block):
         first_row = pl.multiple_of(lax.rem(block, n_gcol) * wide_two, wide_two)
@@ -232,7 +270,7 @@
             moved = jnp.dot(table, field, preferred_element_type=jnp.float32).astype(jnp.bfloat16)
             reals.append(moved[:wide_two])
             imags.append(moved[wide_two:])
-        listed = points[pl.ds(block, 1), :]
+        listed = listed_points(block)
         spot = (listed & (width - 1)) * wide_two + ((listed >> 7) & (wide_two - 1))
         chosen = jnp.where(
             lax.broadcasted_iota(jnp.int32, (width * wide_two, count), 0) == spot, 1.0, 0.0
@@ -381,14 +419,12 @@
     col_count = slab_index.size // (n_pair * blocks)
     if (planes, pairs, n_pair, pair_bands.shape[0], row_count + col_count) != (8, 32, 2, 1, BLOCK_ROWS):
         return on_device_general(valence, conduction, pair_bands, e_val, e_cond, g_index, slab_index)
-    rows = g_index.reshape(n_pair, n_grow, n_gcol, -1).transpose(1, 2, 0, 3)
-    cols = slab_index.reshape(n_gcol, n_pair, n_grow, -1).transpose(2, 0, 1, 3)
-    points = jnp.concatenate([rows, cols], axis=3).reshape(blocks, -1)
     lanes = pairs * planes
     half = BLOCK_ROWS // 2
     width = 4 * pairs
     vmem = pl.BlockSpec(memory_space=pltpu.VMEM)
     smem = pl.BlockSpec(memory_space=pltpu.SMEM)
+    hbm = pl.BlockSpec(memory_space=pltpu.HBM)
     sem = pltpu.SemaphoreType.DMA
     bf16 = jnp.bfloat16
     return pl.pallas_call(
@@ -396,11 +432,17 @@
         out_shape=jax.ShapeDtypeStruct(
             (2, n_gcol * row_count, n_pair * n_grow * col_count), jnp.float32
         ),
-        in_specs=[smem, smem, smem, pl.BlockSpec(memory_space=pl.ANY), vmem, vmem, vmem],
+        in_specs=[hbm, hbm, smem, hbm, hbm, hbm, hbm, hbm],
         out_specs=vmem,
         scratch_shapes=[
+            pltpu.SMEM(pair_bands.shape, jnp.int32),
+            pltpu.SMEM(e_val.shape, jnp.float32),
+            pltpu.VMEM(conduction.shape, bf16),
+            pltpu.VMEM((g_index.size // 128, 128), jnp.int32),
+            pltpu.VMEM((slab_index.size // 128, 128), jnp.int32),
+            pltpu.VMEM((2 * NGRID, 2 * NGRID), bf16),
             *[pltpu.VMEM((2, bands_all, planes, CHUNK * NGRID), bf16)] * SLOTS,
-            pltpu.VMEM((lanes // 128, 2 * NGRID * PITCH, 128), jnp.float32),
+            *[pltpu.VMEM((lanes // 128, 2 * NGRID * PITCH, 128), jnp.float32)] * 2,
             pltpu.VMEM((2 * NGRID, NGRID, lanes), bf16),
             pltpu.VMEM((4 * lanes, width), bf16),
             pltpu.VMEM((NGRID, 2 * lanes), bf16),
@@ -411,15 +453,19 @@
             pltpu.VMEM((n_pair * col_count, width), bf16),
             pltpu.VMEM((n_pair * n_grow, n_pair * col_count, width), bf16),
             sem((SLOTS,)),
+            sem((6,)),
             sem((blocks,)), sem((blocks,)),
             sem((n_pair * n_gcol,)), sem((n_pair * n_gcol,)),
             sem((n_pair * n_grow,)), sem((n_pair * n_grow,)),
         ],
         compiler_params=pltpu.CompilerParams(
-            collective_id=0, has_side_effects=True, vmem_limit_bytes=52 * 2**20
+            collective_id=0, has_side_effects=True, vmem_limit_bytes=56 * 2**20
         ),
         name="slab",
-    )(pair_bands.reshape(-1), e_val, e_cond, valence, conduction, points, jnp.asarray(fixed_table()))
+    )(
+        pair_bands, e_val, e_cond, valence, conduction,
+        g_index.reshape(-1, 128), slab_index.reshape(-1, 128), jnp.asarray(fixed_table()),
+    )
 
 
 def solution(mesh):

time: 48 us -> 43.8 us (0.912)
  local copies, waits for them, and re-layouts: 5.74 us -> 1.92 us
    unnamed x9 -> x0, local copies, waits for them, and re-layouts: 3.25 us -> none
    reshape x3 -> x0, local copies, waits for them, and re-layouts: 1.58 us -> none  [the longest x1 0.81 us: on_device(): rows = g_index.reshape(n_pair, n_grow, n_gcol, -1).transpose(1, 2, 0, 3)]
    pallas_call x1, local copies, waits for them, and re-layouts: 0.89 us -> 1.92 us  [on_device(): pl.pallas_call(functools.partial(slab_kernel, (n_pair, n_grow, n_gcol), r...]
where the time goes in v3:
time: 43.8 us; the launch traced here: 43.7 us
  Pallas kernels  41.1 us (94%)
  local copies, waits for them, and re-layouts  1.92 us (4%)
  between operations  0.66 us (2%)
    pallas_call x1, Pallas kernels, on_device(): pl.pallas_call(functools.partial(slab_kernel, (n_pair, n_grow, n_gcol), r...  41.1 us
    pallas_call x1, local copies, waits for them, and re-layouts, on_device(): pl.pallas_call(functools.partial(slab_kernel, (n_pair, n_grow, n_gcol), r...  1.92 us

profile of v3, /device:TPU:0, one launch (start us, length us, event | category | flops | bytes accessed | tf_op | source)
XLA Modules:
  0.0 43.7 jit_solution(18278905620193854943)
XLA Ops:
  0.7 41.1 %slab.1 = f32[2,480,64]{2,1,0:T(8,128)} custom-call(s32[1,32]{1,0:T(1,128)} %bands_in.1, f32[64]{0:T(128)} %e_val_in.1, f32[1]{0:T(128)S(6)} %copy.10.e_cond, bf16[2,64,8,16384]{3,2,1,0:T(8,128)(2,1)} %val.1, bf16[2,1,8,16384]{3,2,1,0:T(8,128)(2,1)} %cond_in.1, s32[30,128]{1,0:T(8,128)} %bitcast.2, s32[2,128]{1,0:T(2,128)} %bitcast.3, ...), custom_call_target="tpu_custom_call" | custom-call | tf_op jit(solution)/shard_map/slab/pallas_call | solution.py:430
  41.8 1.9 %copy.9 = f32[2,480,64]{1,2,0:T(8,128)} copy(f32[2,480,64]{2,1,0:T(8,128)} %slab.1) | data formatting | bytes 491520 | tf_op jit(solution)/shard_map/slab/pallas_call | solution.py:430

commit v4 on v3

--- a/solution.py
+++ b/solution.py
@@ -203,7 +203,7 @@
         if chunk + slots - 1 < chunks:
             fetch(chunk + slots - 1).start()
 
-        @pl.loop(0, CHUNK, unroll=4)
+        @pl.loop(0, CHUNK, unroll=8)
         def _(step):
             there = pl.ds(pl.multiple_of(chunk * wide + step * NGRID, NGRID), NGRID)
             here = pl.ds(pl.multiple_of(step * NGRID, NGRID), NGRID)
@@ -271,18 +271,17 @@
             reals.append(moved[:wide_two])
             imags.append(moved[wide_two:])
         listed = listed_points(block)
+        listed = jnp.transpose(jnp.broadcast_to(listed, (8, count)))[:, :1]
         spot = (listed & (width - 1)) * wide_two + ((listed >> 7) & (wide_two - 1))
         chosen = jnp.where(
-            lax.broadcasted_iota(jnp.int32, (width * wide_two, count), 0) == spot, 1.0, 0.0
+            lax.broadcasted_iota(jnp.int32, (count, width * wide_two), 1) == spot, 1.0, 0.0
         ).astype(jnp.bfloat16)
         wave = jnp.where(
-            lax.broadcasted_iota(jnp.int32, (NGRID, count), 0) == (listed >> 14), 1.0, 0.0
+            lax.broadcasted_iota(jnp.int32, (count, NGRID), 1) == (listed >> 14), 1.0, 0.0
         ).astype(jnp.bfloat16)
 
         def choose(mask, field):
-            return lax.dot_general(
-                mask, field, (((0,), (0,)), ((), ())), preferred_element_type=jnp.float32
-            )
+            return jnp.dot(mask, field, preferred_element_type=jnp.float32)
 
         re = choose(chosen, jnp.concatenate(reals, axis=0))
         im = choose(chosen, jnp.concatenate(imags, axis=0))
@@ -309,7 +308,7 @@
 
     pl.semaphore_wait(barrier, greeted)
 
-    @pl.loop(1, blocks, unroll=3)
+    @pl.loop(1, blocks, unroll=5)
     def _(distance):
         sums[distance] = partial_sums(lax.rem(me + distance, blocks)).astype(jnp.bfloat16)
         sum_copy(distance).start()

time: 43.8 us -> 41.5 us (0.947)
  Pallas kernels: 41.1 us -> 38.7 us
    pallas_call x1, Pallas kernels: 41.1 us -> 38.7 us  [on_device(): pl.pallas_call(functools.partial(slab_kernel, (n_pair, n_grow, n_gcol), r...]
where the time goes in v4:
time: 41.5 us; the launch traced here: 41.3 us
  Pallas kernels  38.7 us (93%)
  local copies, waits for them, and re-layouts  1.92 us (5%)
  between operations  0.66 us (2%)
    pallas_call x1, Pallas kernels, on_device(): pl.pallas_call(functools.partial(slab_kernel, (n_pair, n_grow, n_gcol), r...  38.7 us
    pallas_call x1, local copies, waits for them, and re-layouts, on_device(): pl.pallas_call(functools.partial(slab_kernel, (n_pair, n_grow, n_gcol), r...  1.92 us

profile of v4, /device:TPU:0, one launch (start us, length us, event | category | flops | bytes accessed | tf_op | source)
XLA Modules:
  0.0 41.3 jit_solution(6195098794521338305)
XLA Ops:
  0.7 38.7 %slab.1 = f32[2,480,64]{2,1,0:T(8,128)} custom-call(s32[1,32]{1,0:T(1,128)} %bands_in.1, f32[64]{0:T(128)} %e_val_in.1, f32[1]{0:T(128)S(6)} %copy.10.e_cond, bf16[2,64,8,16384]{3,2,1,0:T(8,128)(2,1)} %val.1, bf16[2,1,8,16384]{3,2,1,0:T(8,128)(2,1)} %cond_in.1, s32[30,128]{1,0:T(8,128)} %bitcast.2, s32[2,128]{1,0:T(2,128)} %bitcast.3, ...), custom_call_target="tpu_custom_call" | custom-call | tf_op jit(solution)/shard_map/slab/pallas_call | solution.py:429
  39.4 1.9 %copy.9 = f32[2,480,64]{1,2,0:T(8,128)} copy(f32[2,480,64]{2,1,0:T(8,128)} %slab.1) | data formatting | bytes 491520 | tf_op jit(solution)/shard_map/slab/pallas_call | solution.py:429

commit v5 on v4

--- a/solution.py
+++ b/solution.py
@@ -358,7 +358,7 @@
     row_in[row_slot] = row_out[pair_at]
     for _, source in col_copies:
         arrival(col_out, col_in.at[source], col_send.at[0], col_recv.at[source]).wait_recv()
-    lane = lax.broadcasted_iota(jnp.int32, (out.shape[2], 4 * pairs), 1)
+    lane = lax.broadcasted_iota(jnp.int32, (out.shape[1], 4 * pairs), 1)
     tables = {}
     for one in range(n_pair):
         pieces = []
@@ -382,16 +382,20 @@
         for one in range(n_pair)
     ]
     rows = jnp.concatenate(rows, axis=1)
-    for low in range(2):
-        for part in range(2):
+    for part in range(2):
+        made = []
+        for low in range(2):
             table = jnp.concatenate([tables[one, low, part] for one in range(n_pair)], axis=1)
-            made = lax.dot_general(
-                rows, table, (((1,), (1,)), ((), ())), preferred_element_type=jnp.float32
+            made.append(
+                lax.dot_general(
+                    table, rows, (((1,), (1,)), ((), ())), preferred_element_type=jnp.float32
+                )
             )
-            kept = min(half, row_count - low * half)
-            for gcol in range(n_gcol):
+        for gcol in range(n_gcol):
+            for low in range(2):
+                kept = min(half, row_count - low * half)
                 start = gcol * row_count + low * half
-                out[part, start : start + kept, :] = made[gcol * half : gcol * half + kept]
+                out[part, :, start : start + kept] = made[low][:, gcol * half : gcol * half + kept]
     for distance in range(1, blocks):
         sum_copy(distance).wait_send()
     for copy, _ in col_copies + row_copies:
@@ -426,10 +430,10 @@
     hbm = pl.BlockSpec(memory_space=pltpu.HBM)
     sem = pltpu.SemaphoreType.DMA
     bf16 = jnp.bfloat16
-    return pl.pallas_call(
+    made = pl.pallas_call(
         functools.partial(slab_kernel, (n_pair, n_grow, n_gcol), row_count),
         out_shape=jax.ShapeDtypeStruct(
-            (2, n_gcol * row_count, n_pair * n_grow * col_count), jnp.float32
+            (2, n_pair * n_grow * col_count, n_gcol * row_count), jnp.float32
         ),
         in_specs=[hbm, hbm, smem, hbm, hbm, hbm, hbm, hbm],
         out_specs=vmem,
@@ -465,6 +469,7 @@
         pair_bands, e_val, e_cond, valence, conduction,
         g_index.reshape(-1, 128), slab_index.reshape(-1, 128), jnp.asarray(fixed_table()),
     )
+    return jnp.transpose(made, (0, 2, 1))
 
 
 def solution(mesh):

time: 41.5 us -> 41.3 us (level)
    pallas_call x1 -> x0, local copies, waits for them, and re-layouts: 1.92 us -> none  [on_device(): pl.pallas_call(functools.partial(slab_kernel, (n_pair, n_grow, n_gcol), r...]
    unnamed x0 -> x1, local copies, waits for them, and re-layouts: none -> 1.67 us
where the time goes in v5:
time: 41.3 us; the launch traced here: 41.1 us
  Pallas kernels  38.8 us (94%)
  local copies, waits for them, and re-layouts  1.67 us (4%)
  between operations  0.66 us (2%)
    pallas_call x1, Pallas kernels, on_device(): pl.pallas_call(functools.partial(slab_kernel, (n_pair, n_grow, n_gcol), r...  38.8 us
    unnamed x1, local copies, waits for them, and re-layouts  1.67 us

profile of v5, /device:TPU:0, one launch (start us, length us, event | category | flops | bytes accessed | tf_op | source)
XLA Modules:
  0.0 41.1 jit_solution(3111358566256512359)
XLA Ops:
  0.7 38.8 %slab.1 = f32[2,64,480]{2,1,0:T(8,128)} custom-call(s32[1,32]{1,0:T(1,128)} %bands_in.1, f32[64]{0:T(128)} %e_val_in.1, f32[1]{0:T(128)S(6)} %copy.10.e_cond, bf16[2,64,8,16384]{3,2,1,0:T(8,128)(2,1)} %val.1, bf16[2,1,8,16384]{3,2,1,0:T(8,128)(2,1)} %cond_in.1, s32[30,128]{1,0:T(8,128)} %bitcast.4, s32[2,128]{1,0:T(2,128)} %bitcast.5, ...), custom_call_target="tpu_custom_call" | custom-call | tf_op jit(solution)/shard_map/slab/pallas_call | solution.py:433
  39.4 1.7 %copy.11 = f32[2,480,64]{1,2,0:T(8,128)} copy(f32[2,480,64]{1,2,0:T(8,128)} %bitcast.3) | data formatting | bytes 491520
